TPU v7x, 256 devices: a whole 4x4x8 slice. The times are simulated.
256 devices in a mesh: rows: 32 (over y, x, core), cols: 8 (over z).
Axes of the slice: x: 4, y: 4, z: 8, core: 2. Of those that a mesh axis runs over, the one named last changes fastest.
Arguments:
- latent: float32 [2048, 16384], P('rows', 'cols'), may hold values from -3 to 3
- counts: int32 [2048, 16384], P('rows', 'cols'), may hold values from 0 to 39
- exposure: int32 [2048, 16384], P('rows', 'cols'), may hold values from 1 to 32
Outputs:
- newton_step: float32 [2048, 16384], P('rows', 'cols')
- residual: float32 [2048, 16384], P('rows', 'cols')
- direction: float32 [2048, 16384], P('rows', 'cols')
All inputs are finite; a program needn't handle non-finite values.
Results may differ from a plain program's by a relative error of at most 0.0003.
Values sent between devices are 32-bit elements; how exact they have to be, the bound alone decides.
No kernel may reach another device: no remote copies, remote signals or barrier semaphores. Data moves between devices by JAX's collectives and lax.ppermute only.
A program may use at most 128 MiB of HBM per device.

v0:
```python
import math
import jax
import jax.numpy as jnp
from jax import lax
from jax.sharding import PartitionSpec as P

dispersion = 4.0
prior_scale = 0.25
kappa_sq = 0.05
weight_shift = 1.0
highest = lax.Precision.HIGHEST


def extended(cells, sides, width):
    for axis, dim in sides:
        count = lax.axis_size(axis)
        ends = count - 1
        head = lax.slice_in_dim(cells, 0, width, axis=dim)
        tail = lax.slice_in_dim(cells, cells.shape[dim] - width, cells.shape[dim], axis=dim)
        cells = jnp.concatenate(
            [
                lax.ppermute(tail, axis, [(i, (i + 1) % count) for i in range(ends)]),
                cells,
                lax.ppermute(head, axis, [((i + 1) % count, i) for i in range(ends)]),
            ],
            axis=dim,
        )
    return cells


def dft_table(length):
    index_line = lax.iota(jnp.int32, length)
    product = index_line[:, None] * index_line[None, :] % length
    angle = 2.0 * math.pi / length * product.astype(jnp.float32)
    return (jnp.cos(angle), jnp.sin(angle))


def twiddle_table(outer_len, inner_len):
    product = lax.iota(jnp.int32, outer_len)[:, None] * lax.iota(jnp.int32, inner_len)[None, :]
    angle = 2.0 * math.pi / (outer_len * inner_len) * product.astype(jnp.float32)
    return (jnp.cos(angle), jnp.sin(angle))


def left_apply(table, data):
    return jnp.dot(table, data, precision=highest)


def middle_apply(table, data):
    return jnp.einsum("ka,lab->lkb", table, data, precision=highest)


def last_apply(data, table):
    line_rows, outer_len, inner_len = data.shape
    flat = jnp.dot(data.reshape(line_rows * outer_len, inner_len), table, precision=highest)
    return flat.reshape(line_rows, outer_len, inner_len)


def split_lengths(total_cols):
    inner_len = math.gcd(total_cols, 128)
    return (total_cols // inner_len, inner_len)


def columns_forward(real_part, imag_part):
    line_rows, total_cols = real_part.shape
    outer_len, inner_len = split_lengths(total_cols)
    outer_cos, outer_sin = dft_table(outer_len)
    inner_cos, inner_sin = dft_table(inner_len)
    twist_cos, twist_sin = twiddle_table(outer_len, inner_len)
    real_cube = real_part.reshape(line_rows, outer_len, inner_len)
    imag_cube = imag_part.reshape(line_rows, outer_len, inner_len)
    section_real = middle_apply(outer_cos, real_cube) + middle_apply(outer_sin, imag_cube)
    section_imag = middle_apply(outer_cos, imag_cube) - middle_apply(outer_sin, real_cube)
    turned_real = section_real * twist_cos + section_imag * twist_sin
    turned_imag = section_imag * twist_cos - section_real * twist_sin
    final_real = last_apply(turned_real, inner_cos) + last_apply(turned_imag, inner_sin)
    final_imag = last_apply(turned_imag, inner_cos) - last_apply(turned_real, inner_sin)
    return (final_real.reshape(line_rows, total_cols), final_imag.reshape(line_rows, total_cols))


def columns_inverse(real_part, imag_part):
    line_rows, total_cols = real_part.shape
    outer_len, inner_len = split_lengths(total_cols)
    outer_cos, outer_sin = dft_table(outer_len)
    inner_cos, inner_sin = dft_table(inner_len)
    twist_cos, twist_sin = twiddle_table(outer_len, inner_len)
    real_cube = real_part.reshape(line_rows, outer_len, inner_len)
    imag_cube = imag_part.reshape(line_rows, outer_len, inner_len)
    section_real = last_apply(real_cube, inner_cos) - last_apply(imag_cube, inner_sin)
    section_imag = last_apply(imag_cube, inner_cos) + last_apply(real_cube, inner_sin)
    turned_real = section_real * twist_cos - section_imag * twist_sin
    turned_imag = section_imag * twist_cos + section_real * twist_sin
    final_real = middle_apply(outer_cos, turned_real) - middle_apply(outer_sin, turned_imag)
    final_imag = middle_apply(outer_cos, turned_imag) + middle_apply(outer_sin, turned_real)
    return (final_real.reshape(line_rows, total_cols), final_imag.reshape(line_rows, total_cols))


def inverse_symbol(row_freq, col_freq, band_rows, total_cols):
    row_sine = jnp.sin(math.pi * row_freq.astype(jnp.float32) / band_rows)
    col_sine = jnp.sin(math.pi * col_freq.astype(jnp.float32) / total_cols)
    inner_term = kappa_sq + 4.0 * row_sine * row_sine + 4.0 * col_sine * col_sine
    symbol = prior_scale * inner_term * inner_term + weight_shift
    quarter = total_cols // 4
    retained = (col_freq < quarter) | (col_freq > total_cols - quarter)
    weight = jnp.where(retained, 1.0 / symbol, 1.0)
    return weight / float(band_rows * total_cols)


def frequency_of(position, outer_len, inner_len):
    return position // inner_len + outer_len * (position % inner_len)


def precondition(grid_field):
    band_rows, block_cols = grid_field.shape
    col_parts = lax.axis_size("cols")
    col_index = lax.axis_index("cols")
    total_cols = block_cols * col_parts
    outer_len, inner_len = split_lengths(total_cols)
    row_cos, row_sin = dft_table(band_rows)
    spectrum = jnp.stack([left_apply(row_cos, grid_field), -left_apply(row_sin, grid_field)])
    whole_lines = lax.all_to_all(spectrum, "cols", split_axis=1, concat_axis=2, tiled=True)
    line_rows = band_rows // col_parts
    spec_real, spec_imag = columns_forward(whole_lines[0], whole_lines[1])
    row_freq = col_index * line_rows + lax.iota(jnp.int32, line_rows)
    col_freq = frequency_of(lax.iota(jnp.int32, total_cols), outer_len, inner_len)
    spectral_scale = inverse_symbol(row_freq[:, None], col_freq[None, :], band_rows, total_cols)
    back_real, back_imag = columns_inverse(spec_real * spectral_scale, spec_imag * spectral_scale)
    blocks = lax.all_to_all(
        jnp.stack([back_real, back_imag]), "cols", split_axis=2, concat_axis=1, tiled=True
    )
    return left_apply(row_cos, blocks[0]) - left_apply(row_sin, blocks[1])


def prior_apply(grid_field):
    padded = extended(grid_field, (("rows", 0), ("cols", 1)), 2)
    row_count, col_count = grid_field.shape

    def offset_view(shift_row, shift_col):
        return padded[
            2 + shift_row : 2 + shift_row + row_count, 2 + shift_col : 2 + shift_col + col_count
        ]

    centre = kappa_sq + 4.0
    nearest = offset_view(1, 0) + offset_view(-1, 0) + offset_view(0, 1) + offset_view(0, -1)
    diagonal = offset_view(1, 1) + offset_view(1, -1) + offset_view(-1, 1) + offset_view(-1, -1)
    distant = offset_view(2, 0) + offset_view(-2, 0) + offset_view(0, 2) + offset_view(0, -2)
    return prior_scale * (
        (centre * centre + 4.0) * grid_field - 2.0 * centre * nearest + 2.0 * diagonal + distant
    )


def on_device(latent, counts, exposure):
    mean_rate = exposure.astype(jnp.float32) * jnp.exp(latent)
    fisher = dispersion * mean_rate / (dispersion + mean_rate)
    score = (counts.astype(jnp.float32) - mean_rate) * dispersion / (dispersion + mean_rate)
    gradient = score - prior_apply(latent)
    first_search = precondition(gradient)
    first_product = lax.psum(jnp.sum(gradient * first_search), ("rows", "cols"))
    image = prior_apply(first_search) + fisher * first_search
    curvature = lax.psum(jnp.sum(first_search * image), ("rows", "cols"))
    step_size = first_product / curvature
    residual = gradient - step_size * image
    next_search = precondition(residual)
    next_product = lax.psum(jnp.sum(residual * next_search), ("rows", "cols"))
    newton_step = step_size * first_search
    direction = next_search + next_product / first_product * first_search
    return (newton_step, residual, direction)


def solution(mesh):
    placed = (P("rows", "cols"), P("rows", "cols"), P("rows", "cols"))
    return jax.shard_map(
        on_device,
        mesh=mesh,
        in_specs=placed,
        out_specs=(P("rows", "cols"), P("rows", "cols"), P("rows", "cols")),
        check_vma=False,
    )
```

profile of v0, /device:TPU:1, one launch (start us, length us, event | category | flops | bytes accessed | tf_op | source)
XLA Modules:
  0.0 564.2 jit_solution(15677637600210697787)
XLA Ops:
  1.5 5.1 collective-permute-start
  6.7 1.9 collective-permute-start.1
  10.6 1.3 collective-permute-start.2
  11.9 4.0 collective-permute-start.3
  17.0 1.5 pad_maximum_fusion.4
  18.4 2.9 fusion.34
  22.8 1.8 copy.128
  24.6 9.9 %all-to-all-start = ((f32[2,64,2048]{2,0,1:T(2,128)}), f32[2,64,2048]{2,0,1:T(2,128)S(1)}, u32[]{:S(2)}, u32[]{:S(2)}) async-start(f32[2,64,2048]{2,0,1:T(2,128)} %copy.128), calls=%async_computation | async-start | bytes 2097152 | tf_op jit(solution)/shard_map/all_to_all | solution.py:120
  35.6 27.9 %all-to-all-done = f32[2,64,2048]{2,0,1:T(2,128)S(1)} async-done(((f32[2,64,2048]{2,0,1:T(2,128)}), f32[2,64,2048]{2,0,1:T(2,128)S(1)}, u32[]{:S(2)}, u32[]{:S(2)}) %all-to-all-start) | async-done | bytes 1048608 | tf_op jit(solution)/shard_map/all_to_all | solution.py:120
  64.3 1.1 fusion.102
  65.4 1.1 fusion.104
  66.6 1.1 fusion.12
  67.7 1.1 fusion.13
  68.8 1.2 fusion.54
  70.0 1.2 fusion.53
  71.2 1.3 fusion.10
  73.4 1.8 fusion.11
  83.7 14.7 %copy.146 = f32[2,8,16384]{1,0,2:T(2,128)} copy(f32[2,8,16384]{2,1,0:T(8,128)S(1)} %pad_maximum_fusion.1) | data formatting | bytes 2097152 | tf_op jit(solution)/shard_map/stack | solution.py:128
  98.4 28.3 %reshape.237 = f32[8,1,32768]{2,1,0:T(1,128)S(1)} reshape(f32[16384,2,8]{2,1,0:T(2,128)} %bitcast.148) | data formatting | bytes 2097152
  126.7 31.4 %all_to_all.60 = f32[8,1,32768]{2,1,0:T(1,128)S(1)} all-to-all(f32[8,1,32768]{2,1,0:T(1,128)S(1)} %reshape.237), channel_id=1, replica_groups=mesh['rows'=32,'cols'=8] {'cols'}, dimensions={0} | all-to-all | bytes 2097152 | tf_op jit(solution)/shard_map/all_to_all | solution.py:127
  158.7 3.2 reduce
  161.9 32.3 %reshape.238 = f32[16384,2,8]{2,1,0:T(2,128)} reshape(f32[8,32768]{1,0:T(8,128)S(1)} %reduce) | data formatting | bytes 2097152
  194.2 13.2 %copy.194 = f32[2,8,8,2048]{3,2,1,0:T(8,128)S(1)} copy(f32[2,8,8,2048]{1,0,3,2:T(2,128)} %bitcast.149) | data formatting | bytes 2097152 | tf_op jit(solution)/shard_map/all_to_all | solution.py:127
  209.4 1.9 collective-permute-start.5
  211.3 2.4 collective-permute-start.4
  213.8 2.6 collective-permute-done.4
  216.5 1.3 collective-permute-start.6
  217.8 4.0 collective-permute-start.7
  223.1 1.8 multiply_reduce_fusion.1
  224.9 79.0 %all-reduce = (f32[]{:T(128)}, f32[]{:T(128)}) all-reduce(f32[]{:T(128)} %get-tuple-element.4, f32[]{:T(128)} %get-tuple-element.3), channel_id=1, replica_groups=mesh['rows'=32,'cols'=8] {'rows','cols'}, use_global_device_ids=true, to_apply=%region_1.2 | all-reduce | flops 2 | bytes 16 | tf_op jit(solution)/shard_map/psum | solution.py:157
  307.6 31.7 %all_to_all.61 = f32[2,64,2048]{2,0,1:T(2,128)S(1)} all-to-all(f32[2,64,2048]{2,0,1:T(2,128)S(1)} %copy.150), channel_id=1, replica_groups=mesh['rows'=32,'cols'=8] {'cols'}, dimensions={1} | all-to-all | bytes 2097152 | tf_op jit(solution)/shard_map/all_to_all | solution.py:120
  340.2 1.1 fusion.90
  341.4 1.1 fusion.92
  342.5 1.1 fusion.6
  343.6 1.1 fusion.7
  344.7 1.2 fusion.58
  345.9 1.2 fusion.57
  347.1 1.3 fusion.4
  349.3 1.3 fusion.5
  356.9 1.9 stack_reshape.15
  361.1 14.7 %copy.166 = f32[2,8,16384]{1,0,2:T(2,128)} copy(f32[2,8,16384]{2,1,0:T(8,128)S(1)} %pad_maximum_fusion.3) | data formatting | bytes 2097152 | tf_op jit(solution)/shard_map/stack | solution.py:128
  375.8 28.3 %reshape.239 = f32[8,1,32768]{2,1,0:T(1,128)S(1)} reshape(f32[16384,2,8]{2,1,0:T(2,128)} %bitcast.150) | data formatting | bytes 2097152
  404.1 28.8 %all_to_all.62 = f32[8,1,32768]{2,1,0:T(1,128)} all-to-all(f32[8,1,32768]{2,1,0:T(1,128)S(1)} %reshape.239), channel_id=1, replica_groups=mesh['rows'=32,'cols'=8] {'cols'}, dimensions={0} | all-to-all | bytes 2097152 | tf_op jit(solution)/shard_map/all_to_all | solution.py:127
  432.9 4.4 reduce.1
  437.3 32.1 %reshape.240 = f32[16384,2,8]{2,1,0:T(2,128)} reshape(f32[8,32768]{1,0:T(8,128)S(1)} %reduce.1) | data formatting | bytes 2097152
  469.4 13.2 %copy.195 = f32[2,8,8,2048]{3,2,1,0:T(8,128)S(1)} copy(f32[2,8,8,2048]{1,0,3,2:T(2,128)} %bitcast.151) | data formatting | bytes 2097152 | tf_op jit(solution)/shard_map/all_to_all | solution.py:127
  483.6 1.6 multiply_reduce_fusion
  485.2 76.5 %psum.23 = f32[]{:T(128)} all-reduce(f32[]{:T(128)} %get-tuple-element.30), channel_id=1, replica_groups=mesh['rows'=32,'cols'=8] {'rows','cols'}, use_global_device_ids=true, to_apply=%region_5.6 | all-reduce | flops 1 | bytes 8 | tf_op jit(solution)/shard_map/psum | solution.py:163
  (75 shorter events, 35.3 us)
Async XLA Ops:
  1.5 8.2 %collective-permute-start = (f32[2,2048]{1,0:T(2,128)S(1)}, f32[2,2048]{1,0:T(2,128)S(1)}, u32[]{:S(2)}, u32[]{:S(2)}) collective-permute-start(f32[2,2048]{1,0:T(2,128)S(1)} %get-tuple-element.28), channel_id=1, source_target_pairs={{8,0},{16,8},{24,16},{32,24},{40,32},{48,40},{56,48},{64,56},{72,6... | collective-permute-start | bytes 49160 | tf_op jit(solution)/shard_map/ppermute | solution.py:24
  6.7 3.1 collective-permute-start.1
  10.6 5.3 collective-permute-start.2
  11.9 5.0 collective-permute-start.3
  24.6 38.8 %all-to-all-start = ((f32[2,64,2048]{2,0,1:T(2,128)}), f32[2,64,2048]{2,0,1:T(2,128)S(1)}, u32[]{:S(2)}, u32[]{:S(2)}) async-start(f32[2,64,2048]{2,0,1:T(2,128)} %copy.128), calls=%async_computation | async-start | bytes 2097152 | tf_op jit(solution)/shard_map/all_to_all | solution.py:120
  194.2 28.9 %copy-start = (f32[64,2048]{1,0:T(8,128)S(1)}, f32[64,2048]{1,0:T(8,128)}, u32[]{:S(2)}) copy-start(f32[64,2048]{1,0:T(8,128)} %param.3) | copy-start | bytes 1572868
  194.2 28.9 %copy-start.2 = (s32[64,2048]{1,0:T(8,128)S(1)}, s32[64,2048]{1,0:T(8,128)}, u32[]{:S(2)}) copy-start(s32[64,2048]{1,0:T(8,128)} %param.5) | copy-start | bytes 1572868
  209.4 4.3 collective-permute-start.5
  211.3 5.1 collective-permute-start.4
  216.5 5.3 collective-permute-start.6
  217.8 5.0 collective-permute-start.7
  305.3 178.3 %copy-start.1 = (f32[64,2048]{1,0:T(8,128)}, f32[64,2048]{1,0:T(8,128)S(1)}, u32[]{:S(2)}) copy-start(f32[64,2048]{1,0:T(8,128)S(1)} %multiply_subtract_fusion.2) | copy-start | bytes 1572868
where the time goes:
time: 569 us; the launch traced here: 564 us
  blocking collectives  247 us (43%)
  local copies, waits for them, and re-layouts  189 us (33%)
  matrix products  40.4 us (7%)
  waiting for transfers between devices  32.6 us (6%)
  starting transfers between devices  31.8 us (6%)
  other arithmetic  19.3 us (3%)
    unnamed x11, local copies, waits for them, and re-layouts  122 us
    psum x1, blocking collectives, on_device(): first_product = lax.psum(jnp.sum(gradient * first_search), ('rows', 'cols'))  79 us
    psum x1, blocking collectives, on_device(): next_product = lax.psum(jnp.sum(residual * next_search), ('rows', 'cols'))  76.5 us
    all_to_all x2, blocking collectives, precondition(): lax.all_to_all(jnp.stack([back_real, back_imag]), 'cols', split_axis=2, c...  60.2 us
    another operation x6, local copies, waits for them, and re-layouts, precondition(): jnp.stack([back_real, back_imag])  32.4 us
    all_to_all x1, blocking collectives, precondition(): lax.all_to_all(spectrum, 'cols', split_axis=1, concat_axis=2, tiled=True)  31.7 us
    all_to_all x1, waiting for transfers between devices, precondition(): lax.all_to_all(spectrum, 'cols', split_axis=1, concat_axis=2, tiled=True)  27.9 us
    all_to_all x3, local copies, waits for them, and re-layouts, precondition(): lax.all_to_all(jnp.stack([back_real, back_imag]), 'cols', split_axis=2, c...  27 us
  transfers between devices with their start and end apart: 9, of which 5 were waited for; matrix products, arithmetic and copies ran while one was open for 0% of the time, Pallas kernels for 0%

commit v1 on v0

--- a/solution.py
+++ b/solution.py
@@ -117,7 +117,10 @@
     outer_len, inner_len = split_lengths(total_cols)
     row_cos, row_sin = dft_table(band_rows)
     spectrum = jnp.stack([left_apply(row_cos, grid_field), -left_apply(row_sin, grid_field)])
-    whole_lines = lax.all_to_all(spectrum, "cols", split_axis=1, concat_axis=2, tiled=True)
+    whole_lines = jnp.concatenate(
+        lax.all_to_all(jnp.stack(jnp.split(spectrum, lax.axis_size("cols"), axis=1)), "cols", 0, 0),
+        axis=2,
+    )
     line_rows = band_rows // col_parts
     spec_real, spec_imag = columns_forward(whole_lines[0], whole_lines[1])
     row_freq = col_index * line_rows + lax.iota(jnp.int32, line_rows)

time: 569 us -> 571 us (level)
  no operation moved by 1% of the time
where the time goes in v1:
time: 571 us; the launch traced here: 567 us
  blocking collectives  248 us (43%)
  local copies, waits for them, and re-layouts  186 us (33%)
  matrix products  40.2 us (7%)
  waiting for transfers between devices  32.7 us (6%)
  starting transfers between devices  31.7 us (6%)
  other arithmetic  24.6 us (4%)
    unnamed x11, local copies, waits for them, and re-layouts  122 us
    psum x1, blocking collectives, on_device(): first_product = lax.psum(jnp.sum(gradient * first_search), ('rows', 'cols'))  79 us
    psum x1, blocking collectives, on_device(): next_product = lax.psum(jnp.sum(residual * next_search), ('rows', 'cols'))  76.6 us
    all_to_all x2, blocking collectives, precondition(): lax.all_to_all(jnp.stack([back_real, back_imag]), 'cols', split_axis=2, c...  60.2 us
    another operation x6, local copies, waits for them, and re-layouts, precondition(): jnp.stack([back_real, back_imag])  32.4 us
    all_to_all x1, blocking collectives, precondition(): lax.all_to_all(jnp.stack(jnp.split(spectrum, lax.axis_size('cols'), axis=...  31.8 us
    all_to_all x1, waiting for transfers between devices, precondition(): lax.all_to_all(jnp.stack(jnp.split(spectrum, lax.axis_size('cols'), axis=...  28 us
    all_to_all x3, local copies, waits for them, and re-layouts, precondition(): lax.all_to_all(jnp.stack([back_real, back_imag]), 'cols', split_axis=2, c...  27 us
  transfers between devices with their start and end apart: 9, of which 5 were waited for; matrix products, arithmetic and copies ran while one was open for 0% of the time, Pallas kernels for 0%

profile of v1, /device:TPU:1, one launch (start us, length us, event | category | flops | bytes accessed | tf_op | source)
XLA Modules:
  0.0 566.8 jit_solution(3623217719526018424)
XLA Ops:
  1.5 5.1 collective-permute-start
  6.7 1.9 collective-permute-start.1
  10.6 1.3 collective-permute-start.2
  11.9 4.0 collective-permute-start.3
  17.0 1.5 pad_maximum_fusion.2
  18.4 3.0 fusion.34
  28.1 9.8 %all-to-all-start = ((f32[8,2,8,2048]{3,2,1,0:T(8,128)}), f32[8,2,8,2048]{3,2,1,0:T(8,128)S(1)}, u32[]{:S(2)}, u32[]{:S(2)}) async-start(f32[8,2,8,2048]{3,2,1,0:T(8,128)} %fusion.98), calls=%async_computation | async-start | bytes 2097152 | tf_op jit(solution)/shard_map/all_to_all | solution.py:121
  39.0 28.0 %all-to-all-done = f32[8,2,8,2048]{3,2,1,0:T(8,128)S(1)} async-done(((f32[8,2,8,2048]{3,2,1,0:T(8,128)}), f32[8,2,8,2048]{3,2,1,0:T(8,128)S(1)}, u32[]{:S(2)}, u32[]{:S(2)}) %all-to-all-start) | async-done | bytes 1048608 | tf_op jit(solution)/shard_map/all_to_all | solution.py:121
  67.5 1.1 fusion.150
  69.0 1.1 fusion.148
  70.1 1.1 fusion.13
  71.2 1.1 fusion.12
  72.4 1.2 fusion.100
  73.6 1.2 fusion.99
  74.8 1.3 fusion.10
  76.9 1.5 fusion.11
  86.9 14.7 %copy.148 = f32[2,8,16384]{1,0,2:T(2,128)} copy(f32[2,8,16384]{2,1,0:T(8,128)S(1)} %pad_maximum_fusion) | data formatting | bytes 2097152 | tf_op jit(solution)/shard_map/stack | solution.py:131
  101.6 28.3 %reshape.247 = f32[8,1,32768]{2,1,0:T(1,128)S(1)} reshape(f32[16384,2,8]{2,1,0:T(2,128)} %bitcast.206) | data formatting | bytes 2097152
  129.9 31.4 %all_to_all.40 = f32[8,1,32768]{2,1,0:T(1,128)S(1)} all-to-all(f32[8,1,32768]{2,1,0:T(1,128)S(1)} %reshape.247), channel_id=1, replica_groups=mesh['rows'=32,'cols'=8] {'cols'}, dimensions={0} | all-to-all | bytes 2097152 | tf_op jit(solution)/shard_map/all_to_all | solution.py:130
  161.9 3.2 reduce
  165.1 32.1 %reshape.248 = f32[16384,2,8]{2,1,0:T(2,128)} reshape(f32[8,32768]{1,0:T(8,128)S(1)} %reduce) | data formatting | bytes 2097152
  197.1 13.2 %copy.196 = f32[2,8,8,2048]{3,2,1,0:T(8,128)S(1)} copy(f32[2,8,8,2048]{1,0,3,2:T(2,128)} %bitcast.207) | data formatting | bytes 2097152 | tf_op jit(solution)/shard_map/all_to_all | solution.py:130
  212.4 1.9 collective-permute-start.5
  214.3 2.4 collective-permute-start.4
  216.7 2.6 collective-permute-done.4
  219.4 1.3 collective-permute-start.6
  220.7 4.0 collective-permute-start.7
  226.1 1.8 multiply_reduce_fusion.1
  227.9 79.0 %all-reduce = (f32[]{:T(128)}, f32[]{:T(128)}) all-reduce(f32[]{:T(128)} %get-tuple-element.4, f32[]{:T(128)} %get-tuple-element.3), channel_id=1, replica_groups=mesh['rows'=32,'cols'=8] {'rows','cols'}, use_global_device_ids=true, to_apply=%region_1.2 | all-reduce | flops 2 | bytes 16 | tf_op jit(solution)/shard_map/psum | solution.py:160
  309.8 31.8 %all_to_all.41 = f32[8,2,8,2048]{3,2,1,0:T(8,128)S(1)} all-to-all(f32[8,2,8,2048]{3,2,1,0:T(8,128)S(1)} %fusion.96), channel_id=1, replica_groups=mesh['rows'=32,'cols'=8] {'cols'}, dimensions={0} | all-to-all | bytes 2097152 | tf_op jit(solution)/shard_map/all_to_all | solution.py:121
  342.1 1.1 fusion.138
  343.6 1.1 fusion.136
  344.7 1.1 fusion.7
  345.9 1.1 fusion.6
  347.0 1.2 fusion.104
  348.2 1.2 fusion.103
  349.4 1.3 fusion.4
  351.5 1.3 fusion.5
  352.8 1.3 fusion.133
  359.4 1.9 stack_reshape.15
  363.6 14.7 %copy.168 = f32[2,8,16384]{1,0,2:T(2,128)} copy(f32[2,8,16384]{2,1,0:T(8,128)S(1)} %pad_maximum_fusion.1) | data formatting | bytes 2097152 | tf_op jit(solution)/shard_map/stack | solution.py:131
  378.3 28.3 %reshape.249 = f32[8,1,32768]{2,1,0:T(1,128)S(1)} reshape(f32[16384,2,8]{2,1,0:T(2,128)} %bitcast.208) | data formatting | bytes 2097152
  406.6 28.8 %all_to_all.42 = f32[8,1,32768]{2,1,0:T(1,128)} all-to-all(f32[8,1,32768]{2,1,0:T(1,128)S(1)} %reshape.249), channel_id=1, replica_groups=mesh['rows'=32,'cols'=8] {'cols'}, dimensions={0} | all-to-all | bytes 2097152 | tf_op jit(solution)/shard_map/all_to_all | solution.py:130
  435.4 4.4 reduce.1
  439.8 32.1 %reshape.250 = f32[16384,2,8]{2,1,0:T(2,128)} reshape(f32[8,32768]{1,0:T(8,128)S(1)} %reduce.1) | data formatting | bytes 2097152
  471.9 13.2 %copy.197 = f32[2,8,8,2048]{3,2,1,0:T(8,128)S(1)} copy(f32[2,8,8,2048]{1,0,3,2:T(2,128)} %bitcast.209) | data formatting | bytes 2097152 | tf_op jit(solution)/shard_map/all_to_all | solution.py:130
  486.1 1.6 multiply_reduce_fusion
  487.7 76.6 %psum.23 = f32[]{:T(128)} all-reduce(f32[]{:T(128)} %get-tuple-element.30), channel_id=1, replica_groups=mesh['rows'=32,'cols'=8] {'rows','cols'}, use_global_device_ids=true, to_apply=%region_5.6 | all-reduce | flops 1 | bytes 8 | tf_op jit(solution)/shard_map/psum | solution.py:166
  (89 shorter events, 38.6 us)
Async XLA Ops:
  1.5 8.2 %collective-permute-start = (f32[2,2048]{1,0:T(2,128)S(1)}, f32[2,2048]{1,0:T(2,128)S(1)}, u32[]{:S(2)}, u32[]{:S(2)}) collective-permute-start(f32[2,2048]{1,0:T(2,128)S(1)} %get-tuple-element.28), channel_id=1, source_target_pairs={{8,0},{16,8},{24,16},{32,24},{40,32},{48,40},{56,48},{64,56},{72,6... | collective-permute-start | bytes 49160 | tf_op jit(solution)/shard_map/ppermute | solution.py:24
  6.7 3.1 collective-permute-start.1
  10.6 5.3 collective-permute-start.2
  11.9 5.0 collective-permute-start.3
  28.1 38.9 %all-to-all-start = ((f32[8,2,8,2048]{3,2,1,0:T(8,128)}), f32[8,2,8,2048]{3,2,1,0:T(8,128)S(1)}, u32[]{:S(2)}, u32[]{:S(2)}) async-start(f32[8,2,8,2048]{3,2,1,0:T(8,128)} %fusion.98), calls=%async_computation | async-start | bytes 2097152 | tf_op jit(solution)/shard_map/all_to_all | solution.py:121
  197.1 28.9 %copy-start = (f32[64,2048]{1,0:T(8,128)S(1)}, f32[64,2048]{1,0:T(8,128)}, u32[]{:S(2)}) copy-start(f32[64,2048]{1,0:T(8,128)} %param.3) | copy-start | bytes 1572868
  197.1 28.9 %copy-start.2 = (s32[64,2048]{1,0:T(8,128)S(1)}, s32[64,2048]{1,0:T(8,128)}, u32[]{:S(2)}) copy-start(s32[64,2048]{1,0:T(8,128)} %param.5) | copy-start | bytes 1572868
  212.4 4.3 collective-permute-start.5
  214.3 5.1 collective-permute-start.4
  219.4 5.3 collective-permute-start.6
  220.7 5.0 collective-permute-start.7
  308.2 177.9 %copy-start.1 = (f32[64,2048]{1,0:T(8,128)}, f32[64,2048]{1,0:T(8,128)S(1)}, u32[]{:S(2)}) copy-start(f32[64,2048]{1,0:T(8,128)S(1)} %multiply_subtract_fusion.2) | copy-start | bytes 1572868
